TPU v7x, 32 devices: a whole 2x2x4 slice. The times are simulated.
32 devices in a mesh: seq: 2 (over x), exp: 8 (over z, core), head: 2 (over y).
Axes of the slice: x: 2, y: 2, z: 4, core: 2. Of those that a mesh axis runs over, the one named last changes fastest.
Arguments:
- out_grad: bfloat16 [768, 2048], P(('exp', 'head')), may hold values from -6 to 6
- layer_input: bfloat16 [768, 2048], P(('exp', 'head')), may hold values from -6 to 6
- norm_gain: float32 [2048], replicated, may hold values from 0.5 to 1.5
- routes: int32 [768, 8], P(('exp', 'head')), may hold values from 0 to 15, all different within a row; in each aligned block of 48 rows (0 to 47, 48 to 95, ...) at most 32 rows name the same one
- gates: float32 [768, 8], P(('exp', 'head')), may hold values from 0.02 to 0.3
- gate_pre: bfloat16 [2, 16, 8, 32, 768], P('head', 'exp', None, None, 'seq'), may hold values from -6 to 6
- up_pre: bfloat16 [2, 16, 8, 32, 768], P('head', 'exp', None, None, 'seq'), may hold values from -6 to 6
- w_gate: bfloat16 [16, 2048, 768], P('exp', None, 'seq'), may hold values from -0.125 to 0.125
- w_up: bfloat16 [16, 2048, 768], P('exp', None, 'seq'), may hold values from -0.125 to 0.125
- w_down: bfloat16 [16, 768, 2048], P('exp', 'seq'), may hold values from -0.21875 to 0.21875
- w_out: bfloat16 [4096, 2048], P('head'), may hold values from -0.09375 to 0.09375
Outputs:
- resid_grad: float32 [2, 384, 2048], P('seq', ('exp', 'head'))
- head_grad: bfloat16 [2, 384, 4096], P('seq', 'exp', 'head')
Inputs may be any that keep to these rules, and one draw needn't show every extreme that they name: `routes`: each row names 8 different experts. In each aligned block of 48 rows (the tokens of one device) no expert is named by more than 32 rows, a bound that some block reaches.
All inputs are finite; a program needn't handle non-finite values.
Results may differ from a plain program's by a relative error of at most 0.0095.
Values may be sent and summed in bfloat16 or wider, within the bound.
A program may use at most 64 MiB of HBM per device.

v0:
```python
import jax
import jax.numpy as jnp
from jax import lax
from jax.sharding import PartitionSpec as P


def expert_rows(slot_piece, gate_piece, up_piece, w_gate, w_up, w_down):
    gate_act = gate_piece.astype(jnp.float32)
    up_act = up_piece.astype(jnp.float32)
    d_hidden = jnp.einsum("jgcd,jfd->jgcf", slot_piece, w_down, preferred_element_type=jnp.float32)
    sigmoid_gate = jax.nn.sigmoid(gate_act)
    silu_gate = gate_act * sigmoid_gate
    silu_slope = sigmoid_gate * (1.0 + gate_act * (1.0 - sigmoid_gate))
    d_gate = (d_hidden * up_act * silu_slope).astype(jnp.bfloat16)
    d_up = (d_hidden * silu_gate).astype(jnp.bfloat16)
    partial_value = jnp.einsum("jgcf,jdf->jgcd", d_gate, w_gate, preferred_element_type=jnp.float32)
    partial_value = partial_value + jnp.einsum(
        "jgcf,jdf->jgcd", d_up, w_up, preferred_element_type=jnp.float32
    )
    return partial_value.astype(jnp.bfloat16)


def shards(
    out_grad, layer_input, norm_gain, routes, gates, gate_pre, up_pre, w_gate, w_up, w_down, w_out
):
    experts_here = w_gate.shape[0]
    exp_groups = lax.axis_size("exp")
    capacity = gate_pre.shape[3]
    tok_count = routes.shape[0]
    top_count = routes.shape[1]
    model_width = out_grad.shape[1]
    total_experts = experts_here * exp_groups
    flat_routes = routes.reshape(-1)
    onehot = (flat_routes[:, None] == jnp.arange(total_experts, dtype=jnp.int32)[None, :]).astype(
        jnp.int32
    )
    position = jnp.sum((jnp.cumsum(onehot, axis=0) - 1) * onehot, axis=1)
    target = flat_routes // experts_here
    local_expert = flat_routes % experts_here
    slot_index = (local_expert * exp_groups + target) * capacity + position
    scaled = (
        (gates[:, :, None] * out_grad[:, None, :].astype(jnp.float32))
        .astype(jnp.bfloat16)
        .reshape(-1, model_width)
    )
    outgoing = (
        jnp.zeros((total_experts * capacity, model_width), jnp.bfloat16).at[slot_index].set(scaled)
    )
    outgoing = outgoing.reshape(experts_here, exp_groups, capacity, model_width)
    gate_local = gate_pre[0]
    up_local = up_pre[0]
    received = lax.all_to_all(outgoing, "exp", split_axis=1, concat_axis=1, tiled=True)
    partial_value = expert_rows(received, gate_local, up_local, w_gate, w_up, w_down)
    returned = lax.all_to_all(
        partial_value, "exp", split_axis=1, concat_axis=1, tiled=True
    ).reshape(-1, model_width)
    picked = returned[slot_index].astype(jnp.float32)
    combined = jnp.sum(picked.reshape(tok_count, top_count, model_width), axis=1)
    moe_rows = lax.psum_scatter(
        combined.astype(jnp.bfloat16), "seq", scatter_dimension=0, tiled=True
    ).astype(jnp.float32)
    rows_here = moe_rows.shape[0]
    row_start = lax.axis_index("seq") * rows_here
    inputs = lax.dynamic_slice_in_dim(layer_input, row_start, rows_here, 0).astype(jnp.float32)
    out_rows = lax.dynamic_slice_in_dim(out_grad, row_start, rows_here, 0).astype(jnp.float32)
    inv_rms = lax.rsqrt(jnp.mean(inputs * inputs, axis=1, keepdims=True) + 1e-06)
    normed = inputs * inv_rms
    scaled_grad = moe_rows * norm_gain[None, :]
    resid_grad = out_rows + inv_rms * (
        scaled_grad - normed * jnp.mean(scaled_grad * normed, axis=1, keepdims=True)
    )
    rounded_grad = resid_grad.astype(jnp.bfloat16)
    head_grad = lax.dot_general(
        lax.all_gather(rounded_grad, "head", axis=0, tiled=True),
        w_out,
        (((1,), (1,)), ((), ())),
        preferred_element_type=jnp.float32,
    )
    return (resid_grad[None], head_grad.astype(jnp.bfloat16)[None])


def solution(mesh):
    placed = (
        P(("exp", "head"), None),
        P(("exp", "head"), None),
        P(),
        P(("exp", "head"), None),
        P(("exp", "head"), None),
        P("head", "exp", None, None, "seq"),
        P("head", "exp", None, None, "seq"),
        P("exp", None, "seq"),
        P("exp", None, "seq"),
        P("exp", "seq", None),
        P("head", None),
    )
    return jax.shard_map(
        shards,
        mesh=mesh,
        in_specs=placed,
        out_specs=(P("seq", ("exp", "head"), None), P("seq", "exp", "head")),
        check_vma=False,
    )
```

profile of v0, /device:TPU:0, one launch (start us, length us, event | category | flops | bytes accessed | tf_op | source)
XLA Modules:
  0.0 179.9 jit_solution(5384313151582029321)
XLA Ops:
  7.2 0.0 copy-start
  7.2 0.9 copy.26
  8.1 0.1 eq.31
  8.2 0.1 eq.27
  8.3 0.1 reshape.178
  8.4 0.9 reduce-window.6
  9.3 0.0 copy-start.6
  9.3 0.2 slice_reduce_fusion
  9.5 0.4 copy-done.6
  9.9 1.0 convert_element_type.55
  10.9 1.4 copy.30
  12.2 0.8 mul.112
  13.1 0.8 fusion.37
  13.9 4.5 %scatter_custom_fusion = bf16[512,2048]{1,0:T(8,128)(2,1)} fusion(s32[384]{0:T(512)S(1)} %fusion.39, f32[48,2048]{1,0:T(8,128)S(1)} %convert_element_type.55, f32[384]{0:T(512)S(1)} %mul.112, bf16[]{:T(256)} %constant.55.clone.1), kind=kCustom, calls=%fused_computation.13 | custom fusion | flops 1572864 | bytes 2492418 | tf_op jit(solution)/shard_map/scatter | solution.py:47
  18.4 1.7 copy.31
  20.2 0.0 copy-start.8
  20.2 55.5 %all_to_all.10 = bf16[2,8,32,2048]{3,2,0,1:T(8,128)(2,1)S(1)} all-to-all(bf16[2,8,32,2048]{3,2,0,1:T(8,128)(2,1)S(1)} %copy.31), channel_id=1, replica_groups=mesh['seq'=2,'exp'=8,'head'=2] {'exp'}, dimensions={1} | all-to-all | bytes 4194304 | tf_op jit(solution)/shard_map/all_to_all | solution.py:52
  75.6 0.0 copy-done.8
  75.6 0.0 copy-start.2
  75.6 0.0 copy-start.5
  75.6 1.3 fusion.3
  76.9 0.0 copy-done
  76.9 0.0 copy-done.2
  76.9 0.0 copy-done.5
  76.9 0.0 copy-start.1
  76.9 1.3 fusion.1
  78.3 0.5 copy-done.1
  78.8 1.3 add_convert_fusion
  80.1 1.4 copy.33
  81.6 4.3 %all-to-all-start.1 = ((bf16[2,8,32,2048]{3,2,0,1:T(8,128)(2,1)}), bf16[2,8,32,2048]{3,2,0,1:T(8,128)(2,1)}, u32[]{:S(2)}, u32[]{:S(2)}) async-start(bf16[2,8,32,2048]{3,2,0,1:T(8,128)(2,1)} %copy.33), calls=%async_computation.1 | async-start | bytes 4194304 | tf_op jit(solution)/shard_map/all_to_all | solution.py:54
  85.9 0.0 reduce-scatter.2.cloned.1.call-start
  86.0 49.0 %all-to-all-done.1 = bf16[2,8,32,2048]{3,2,0,1:T(8,128)(2,1)} async-done(((bf16[2,8,32,2048]{3,2,0,1:T(8,128)(2,1)}), bf16[2,8,32,2048]{3,2,0,1:T(8,128)(2,1)}, u32[]{:S(2)}, u32[]{:S(2)}) %all-to-all-start.1) | async-done | bytes 2097184 | tf_op jit(solution)/shard_map/all_to_all | solution.py:54
  135.0 3.1 %copy.34 = bf16[2,8,32,2048]{3,2,1,0:T(8,128)(2,1)} copy(bf16[2,8,32,2048]{3,2,0,1:T(8,128)(2,1)} %all-to-all-done.1) | data formatting | bytes 4194304 | tf_op jit(solution)/shard_map/all_to_all | solution.py:54
  138.1 0.0 copy-start.3
  138.1 0.0 copy-start.7
  138.1 7.0 %gather_fusion = bf16[384,2048]{1,0:T(8,128)(2,1)} fusion(bf16[512,2048]{1,0:T(8,128)(2,1)} %bitcast.62, s32[1024]{0:T(1024)S(1)} %pad_clamp_fusion), kind=kCustom, calls=%fused_computation | custom fusion | bytes 3147264 | tf_op jit(solution)/shard_map/gather | solution.py:57
  145.1 0.0 copy-start.4
  145.1 3.2 %bitcast_reduce_fusion = bf16[48,2048]{1,0:T(8,128)(2,1)} fusion(bf16[384,2048]{1,0:T(8,128)(2,1)} %gather_fusion), kind=kLoop, calls=%fused_computation.14 | loop fusion | flops 688128 | bytes 1769472 | tf_op jit(solution)/shard_map/reduce_sum | solution.py:58
  148.3 0.0 reduce-scatter.2.cloned.1.call-update
  148.3 0.0 copy-done.3
  148.3 0.1 fusion.35
  148.5 9.8 %reduce-scatter.2.cloned.1.call-done = bf16[24,2048]{1,0:T(8,128)(2,1)} async-done(((bf16[48,2048]{1,0:T(8,128)(2,1)}), bf16[24,2048]{1,0:T(8,128)(2,1)}) %reduce-scatter.2.cloned.1.call-update) | async-done | bytes 98320 | tf_op jit(solution)/shard_map/reduce_scatter | solution.py:59
  158.3 0.0 copy-done.7
  158.3 1.1 fusion.31
  159.4 0.0 copy-done.4
  159.4 1.7 fusion.44
  161.1 5.3 %all_gather.3 = bf16[48,2048]{1,0:T(8,128)(2,1)S(1)} all-gather(bf16[24,2048]{1,0:T(8,128)(2,1)S(1)} %get-tuple-element.2), channel_id=1, replica_groups=mesh['seq'=2,'exp'=8,'head'=2] {'head'}, dimensions={0}, use_global_device_ids=true | all-gather | bytes 294912 | tf_op jit(solution)/shard_map/all_gather | solution.py:74
  166.4 6.7 %fusion.6 = bf16[1,48,2048]{2,1,0:T(8,128)(2,1)} fusion(bf16[48,2048]{1,0:T(8,128)(2,1)S(1)} %all_gather.3, bf16[2048,2048]{1,0:T(8,128)(2,1)} %param.21), kind=kOutput, calls=%fused_computation.11 | convolution fusion | flops 402751488 | bytes 8781824 | tf_op jit(solution)/shard_map/dot_general | solution.py:73
  (6 shorter events, 0.1 us)
Async XLA Ops:
  7.2 69.7 %copy-start = (bf16[2,2048,384]{2,1,0:T(8,128)(2,1)S(1)}, bf16[2,2048,384]{2,1,0:T(8,128)(2,1)}, u32[]{:S(2)}) copy-start(bf16[2,2048,384]{2,1,0:T(8,128)(2,1)} %param.18) | copy-start | bytes 9437188
  9.3 0.6 copy-start.6
  20.2 55.5 %copy-start.8 = (bf16[2,384,2048]{2,1,0:T(8,128)(2,1)S(1)}, bf16[2,384,2048]{2,1,0:T(8,128)(2,1)}, u32[]{:S(2)}) copy-start(bf16[2,384,2048]{2,1,0:T(8,128)(2,1)} %param.20) | copy-start | bytes 9437188
  75.6 1.3 copy-start.2
  75.6 1.3 copy-start.5
  76.9 1.9 %copy-start.1 = (bf16[2,2048,384]{2,1,0:T(8,128)(2,1)S(1)}, bf16[2,2048,384]{2,1,0:T(8,128)(2,1)}, u32[]{:S(2)}) copy-start(bf16[2,2048,384]{2,1,0:T(8,128)(2,1)} %param.19) | copy-start | bytes 9437188
  81.6 53.4 %all-to-all-start.1 = ((bf16[2,8,32,2048]{3,2,0,1:T(8,128)(2,1)}), bf16[2,8,32,2048]{3,2,0,1:T(8,128)(2,1)}, u32[]{:S(2)}, u32[]{:S(2)}) async-start(bf16[2,8,32,2048]{3,2,0,1:T(8,128)(2,1)} %copy.33), calls=%async_computation.1 | async-start | bytes 4194304 | tf_op jit(solution)/shard_map/all_to_all | solution.py:54
  85.9 72.4 %reduce-scatter.2.cloned.1.call-start = ((), (), s32[]{:S(2)}) async-start(), calls=%async_computation.3 | async-start | bytes 294912 | tf_op jit(solution)/shard_map/reduce_scatter | solution.py:59
  138.1 10.2 %copy-start.3 = (bf16[48,2048]{1,0:T(8,128)(2,1)S(1)}, bf16[48,2048]{1,0:T(8,128)(2,1)}, u32[]{:S(2)}) copy-start(bf16[48,2048]{1,0:T(8,128)(2,1)} %param.12) | copy-start | bytes 589828
  138.1 20.2 %copy-start.7 = (f32[2048]{0:T(1024)S(1)}, f32[2048]{0:T(1024)}, u32[]{:S(2)}) copy-start(f32[2048]{0:T(1024)} %param.13) | copy-start | bytes 24580
  145.1 14.3 %copy-start.4 = (bf16[48,2048]{1,0:T(8,128)(2,1)S(1)}, bf16[48,2048]{1,0:T(8,128)(2,1)}, u32[]{:S(2)}) copy-start(bf16[48,2048]{1,0:T(8,128)(2,1)} %param.11) | copy-start | bytes 589828
Sparse Core Ops, SparseCore 0:
  148.4 9.8 reduce-scatter.1
where the time goes:
time: 181 us; the launch traced here: 180 us
  blocking collectives  60.7 us (34%)
  waiting for transfers between devices  58.8 us (32%)
  local copies, waits for them, and re-layouts  17.8 us (10%)
  between operations  14.2 us (8%)
  other arithmetic  13.4 us (7%)
  matrix products  10.6 us (6%)
  starting transfers between devices  4.38 us (2%)
    all_to_all x1, blocking collectives, shards(): lax.all_to_all(outgoing, 'exp', split_axis=1, concat_axis=1, tiled=True)  55.5 us
    all_to_all x1, waiting for transfers between devices, shards(): lax.all_to_all(partial_value, 'exp', split_axis=1, concat_axis=1, tiled=T...  49 us
    reduce_scatter x1, waiting for transfers between devices, shards(): lax.psum_scatter(combined.astype(jnp.bfloat16), 'seq', scatter_dimension=...  9.83 us
    gather x1, local copies, waits for them, and re-layouts, shards(): picked = returned[slot_index].astype(jnp.float32)  6.97 us
    dot_general x1, matrix products, shards(): lax.dot_general(lax.all_gather(rounded_grad, 'head', axis=0, tiled=True),...  6.69 us
    all_gather x1, blocking collectives, shards(): lax.all_gather(rounded_grad, 'head', axis=0, tiled=True)  5.28 us
    scatter x1, other arithmetic, shards(): jnp.zeros((total_experts * capacity, model_width), jnp.bfloat16)  4.5 us
    all_to_all x1, starting transfers between devices, shards(): lax.all_to_all(partial_value, 'exp', split_axis=1, concat_axis=1, tiled=T...  4.34 us
  transfers between devices with their start and end apart: 2, of which 2 were waited for; matrix products, arithmetic and copies ran while one was open for 0% of the time, Pallas kernels for 0%

commit v1 on v0

v1 whole, which is shorter than its diff:
```python
import functools

import jax
import jax.numpy as jnp
from jax import lax
from jax.experimental import pallas as pl
from jax.experimental.pallas import tpu as pltpu
from jax.sharding import PartitionSpec as P

MESH = pl.DeviceIdType.MESH
F32 = jnp.float32
BF16 = jnp.bfloat16
NT_DIMS = (((1,), (1,)), ((), ()))
COLUMN_TILES = 4


def dot_nt(a, b):
    return lax.dot_general(a, b, NT_DIMS, preferred_element_type=F32)


def kernel(
    sizes,
    og, li, gain, routes, gates, gp_hbm, up_hbm, wg_hbm, wu_hbm, wd_hbm, wo_hbm,
    resid, head,
    xg, info_src, info_all, gp, up, wg, wu, wd, wo, coef_gate, coef_up, dgate, dup,
    mine, core_rx, sx, x_rx, sz, z_rx, moe, hx, lhs,
    load_sem, z_snd, sib_snd, x_snd, info_snd, core_snd, xs_snd, zs_snd, head_snd,
    xg_rcv, info_rcv, core_rcv, xs_rcv, zs_rcv, head_rcv,
):
    S, E, H, J, T, D, C = sizes
    Z = E // 2
    DS = D // S
    R = T // S
    NT = COLUMN_TILES
    TN = DS // NT
    s = lax.axis_index("seq")
    e = lax.axis_index("exp")
    h = lax.axis_index("head")
    z = e // 2
    c = e % 2
    sib = z * 2 + (1 - c)

    def remote(src, dst, snd, rcv, **where):
        return pltpu.make_async_remote_copy(
            src_ref=src, dst_ref=dst, send_sem=snd, recv_sem=rcv,
            device_id=where, device_id_type=MESH,
        )

    barrier = pltpu.get_barrier_semaphore()
    for k in range(1, E):
        pl.semaphore_signal(barrier, inc=1, device_id={"exp": (e + k) % E}, device_id_type=MESH)
    for k in range(1, S):
        pl.semaphore_signal(barrier, inc=1, device_id={"seq": (s + k) % S}, device_id_type=MESH)
    for k in range(1, H):
        pl.semaphore_signal(barrier, inc=1, device_id={"head": (h + k) % H}, device_id_type=MESH)

    loads = [
        pltpu.make_async_copy(src, dst, load_sem.at[i])
        for i, (src, dst) in enumerate(
            ((gp_hbm, gp), (up_hbm, up), (wd_hbm, wd), (wg_hbm, wg), (wu_hbm, wu), (wo_hbm, wo))
        )
    ]
    for load in loads:
        load.start()
    for q in range(S):
        xg[e, q] = og[:, q * DS:(q + 1) * DS]

    pl.semaphore_wait(barrier, E - 1 + S - 1 + H - 1)

    sent = []

    def start(copy):
        copy.start()
        sent.append(copy)

    def chunk(block, part, snd, **where):
        return remote(xg.at[block, part], xg.at[block, part], snd, xg_rcv.at[block, part], **where)

    for k in range(1, Z):
        start(chunk(e, s, z_snd.at[k], exp=((z + k) % Z) * 2 + c))
    for q in range(S):
        start(chunk(e, q, sib_snd.at[0, q], exp=sib))

    X8 = E * 8
    XP = max(128, X8)
    lane = lax.broadcasted_iota(jnp.int32, (T, XP), 1)
    kind = lane % 8
    expert = (lane // 8) * J + kind % J
    weight = jnp.zeros((T, XP), F32)
    member = jnp.zeros((T, XP), F32)
    for k in range(routes.shape[1]):
        hit = routes[:, k:k + 1] == expert
        weight = weight + jnp.where(hit, gates[:, k:k + 1], 0.0)
        member = jnp.where(hit, 1.0, member)
    earlier = (
        lax.broadcasted_iota(jnp.int32, (T, T), 0) > lax.broadcasted_iota(jnp.int32, (T, T), 1)
    ).astype(F32).astype(BF16)
    position = jnp.dot(earlier, member.astype(BF16), preferred_element_type=F32)
    info = jnp.where(kind < J, weight, jnp.where(member > 0.0, position, -1.0))
    info = jnp.concatenate([info, jnp.zeros((128 - T, XP), F32)], axis=0).T
    info_src[...] = info[:X8].reshape(E, 8, 128)
    for k in range(1, E):
        to = (e + k) % E
        start(remote(info_src.at[to], info_all.at[e], info_snd.at[k], info_rcv.at[e], exp=to))
    info_all[e] = info_src[e]

    for k in range(1, Z):
        block = ((z + k) % Z) * 2 + c
        chunk(block, s, z_snd.at[k], exp=sib).wait_recv()
        for i in range(1, S):
            start(chunk(block, s, x_snd.at[k, i], seq=(s + i) % S))
        start(chunk(block, s, sib_snd.at[k, 0], exp=sib))

    for k in range(1, E):
        frm = (e + k) % E
        remote(info_src.at[frm], info_all.at[frm], info_snd.at[k], info_rcv.at[frm], exp=frm).wait_recv()
    table = info_all[...].reshape(X8, 128)
    if XP > X8:
        table = jnp.concatenate([table, jnp.zeros((XP - X8, 128), F32)], axis=0)
    table = table.T
    loads[0].wait()
    loads[1].wait()
    slot = lax.broadcasted_iota(jnp.int32, (E * T, E * C), 1).astype(F32)
    for j in range(J):
        gate_col = jnp.concatenate([table[:T, b * 8 + j:b * 8 + j + 1] for b in range(E)], axis=0)
        place = []
        for b in range(E):
            col = table[:T, b * 8 + J + j:b * 8 + J + j + 1]
            place.append(jnp.where(col >= 0.0, col + float(b * C), -1.0))
        place = jnp.concatenate(place, axis=0)
        pick = jnp.where(slot == place, 1.0, 0.0).astype(BF16)
        a = jnp.dot(pick, gp[j], preferred_element_type=F32)
        b = jnp.dot(pick, up[j], preferred_element_type=F32)
        sig = jax.nn.sigmoid(a)
        coef_gate[j] = gate_col * b * sig * (1.0 + a * (1.0 - sig))
        coef_up[j] = gate_col * a * sig

    for k in range(1, Z):
        block = ((z + k) % Z) * 2 + c
        for i in range(1, S):
            part = (s + S - i) % S
            chunk(block, part, x_snd.at[k, i], exp=sib).wait_recv()
            start(chunk(block, part, sib_snd.at[k, i], exp=sib))

    for k in range(Z):
        block = ((z + k) % Z) * 2 + (1 - c)
        for i in range(S):
            part = (s + S - i) % S
            chunk(block, part, sib_snd.at[k, i], exp=sib).wait_recv()

    loads[2].wait()
    for j in range(J):
        hidden = None
        for q in range(S):
            term = dot_nt(xg[:, q].reshape(E * T, DS), wd[j, :, q * DS:(q + 1) * DS])
            hidden = term if hidden is None else hidden + term
        dgate[j] = (hidden * coef_gate[j]).astype(BF16)
        dup[j] = (hidden * coef_up[j]).astype(BF16)
    loads[3].wait()
    loads[4].wait()

    def core_copy(n):
        return remote(mine.at[n, 1 - c], core_rx.at[n], core_snd.at[n], core_rcv.at[n], exp=sib)

    def x_copy(n, i):
        to = (s + i) % S
        return remote(sx.at[n, to], x_rx.at[n, i], xs_snd.at[n, i], xs_rcv.at[n, i], seq=to)

    def z_copy(n, k):
        to = (z + k) % Z
        return remote(sz.at[n, to], z_rx.at[n, k], zs_snd.at[n, k], zs_rcv.at[n, k], exp=to * 2 + c)

    def stage_compute(n):
        tiles = []
        for q in range(S):
            cols = slice(q * DS + n * TN, q * DS + (n + 1) * TN)
            acc = None
            for j in range(J):
                term = dot_nt(dgate[j], wg[j, cols, :]) + dot_nt(dup[j], wu[j, cols, :])
                acc = term if acc is None else acc + term
            tiles.append(acc)
        for b in range(E):
            for p in range(S):
                rows = slice(b * T + p * R, b * T + (p + 1) * R)
                mine[n, b % 2, p, b // 2] = jnp.concatenate(
                    [tile[rows] for tile in tiles], axis=0
                ).astype(BF16)
        start(core_copy(n))

    def stage_x(n):
        core_copy(n).wait_recv()
        sx[n] = (mine[n, c].astype(F32) + core_rx[n].astype(F32)).astype(BF16)
        for i in range(1, S):
            start(x_copy(n, i))

    def stage_z(n):
        total = sx[n, s].astype(F32)
        for i in range(1, S):
            x_copy(n, i).wait_recv()
            total = total + x_rx[n, i].astype(F32)
        sz[n] = total.astype(BF16)
        for k in range(1, Z):
            start(z_copy(n, k))

    def stage_end(n):
        total = sz[n, z].astype(F32)
        for k in range(1, Z):
            z_copy(n, k).wait_recv()
            total = total + z_rx[n, k].astype(F32)
        for q in range(S):
            moe[:, q * DS + n * TN:q * DS + (n + 1) * TN] = total[q * R:(q + 1) * R]

    stages = (stage_compute, stage_x, stage_z, stage_end)
    for step in range(NT + len(stages) - 1):
        for i, stage in enumerate(stages):
            if 0 <= step - i < NT:
                stage(step - i)

    def rows_of(ref):
        wide = ref[...].astype(F32)
        mine_rows = wide[:R]
        for p in range(1, S):
            mine_rows = jnp.where(s == p, wide[p * R:(p + 1) * R], mine_rows)
        return mine_rows

    inputs = rows_of(li)
    inv_rms = lax.rsqrt(jnp.mean(inputs * inputs, axis=1, keepdims=True) + 1e-06)
    normed = inputs * inv_rms
    scaled = moe[...] * gain[...]
    full = rows_of(og) + inv_rms * (
        scaled - normed * jnp.mean(scaled * normed, axis=1, keepdims=True)
    )
    resid[...] = full
    hx[h] = jnp.concatenate([full[:, q * DS:(q + 1) * DS] for q in range(S)], axis=0).astype(BF16)
    for k in range(1, H):
        start(remote(hx.at[h], hx.at[h], head_snd.at[k], head_rcv.at[h], head=(h + k) % H))
    for k in range(1, H):
        frm = (h + k) % H
        remote(hx.at[frm], hx.at[frm], head_snd.at[k], head_rcv.at[frm], head=frm).wait_recv()
    parts = [hx[p].astype(F32) for p in range(H)]
    for q in range(S):
        lhs[:, q * DS:(q + 1) * DS] = jnp.concatenate(
            [part[q * R:(q + 1) * R] for part in parts], axis=0
        ).astype(BF16)
    loads[5].wait()
    A = wo.shape[0]
    AT = min(A, 512)
    for a0 in range(0, A, AT):
        head[:, a0:a0 + AT] = dot_nt(lhs[...], wo[a0:a0 + AT, :]).astype(BF16)
    for copy in sent:
        copy.wait_send()


def shards(
    out_grad, layer_input, norm_gain, routes, gates, gate_pre, up_pre, w_gate, w_up, w_down, w_out
):
    S, E, H = lax.axis_size("seq"), lax.axis_size("exp"), lax.axis_size("head")
    T, D = out_grad.shape
    J, F = w_down.shape[:2]
    C = gate_pre.shape[3]
    A = w_out.shape[0]
    Z = E // 2
    DS = D // S
    R = T // S
    NT = COLUMN_TILES
    TN = DS // NT
    gp = gate_pre.reshape(J, E * C, F)
    up = up_pre.reshape(J, E * C, F)
    vmem = pl.BlockSpec(memory_space=pltpu.VMEM)
    hbm = pl.BlockSpec(memory_space=pl.ANY)
    dma = pltpu.SemaphoreType.DMA
    scratch = [
        pltpu.VMEM((E, S, T, DS), BF16),
        pltpu.VMEM((E, 8, 128), F32),
        pltpu.VMEM((E, 8, 128), F32),
        pltpu.VMEM((J, E * C, F), BF16),
        pltpu.VMEM((J, E * C, F), BF16),
        pltpu.VMEM((J, D, F), BF16),
        pltpu.VMEM((J, D, F), BF16),
        pltpu.VMEM((J, F, D), BF16),
        pltpu.VMEM((A, D), BF16),
        pltpu.VMEM((J, E * T, F), F32),
        pltpu.VMEM((J, E * T, F), F32),
        pltpu.VMEM((J, E * T, F), BF16),
        pltpu.VMEM((J, E * T, F), BF16),
        pltpu.VMEM((NT, 2, S, Z, T, TN), BF16),
        pltpu.VMEM((NT, S, Z, T, TN), BF16),
        pltpu.VMEM((NT, S, Z, T, TN), BF16),
        pltpu.VMEM((NT, S, Z, T, TN), BF16),
        pltpu.VMEM((NT, Z, T, TN), BF16),
        pltpu.VMEM((NT, Z, T, TN), BF16),
        pltpu.VMEM((R, D), F32),
        pltpu.VMEM((H, T, DS), BF16),
        pltpu.VMEM((H * R, D), BF16),
        dma((6,)), dma((Z,)), dma((Z, S)), dma((Z, S)), dma((E,)), dma((NT,)),
        dma((NT, S)), dma((NT, Z)), dma((H,)),
        dma((E, S)), dma((E,)), dma((NT,)), dma((NT, S)), dma((NT, Z)), dma((H,)),
    ]
    rows = E * T
    flops = 2 * rows * D * F * J * 3 + 2 * H * R * D * A
    resid, head = pl.pallas_call(
        functools.partial(kernel, (S, E, H, J, T, D, C)),
        out_shape=(
            jax.ShapeDtypeStruct((R, D), F32),
            jax.ShapeDtypeStruct((H * R, A), BF16),
        ),
        in_specs=[vmem] * 5 + [hbm] * 6,
        out_specs=(vmem, vmem),
        scratch_shapes=scratch,
        compiler_params=pltpu.CompilerParams(
            collective_id=0, has_side_effects=True, vmem_limit_bytes=56 * 1024 * 1024
        ),
        cost_estimate=pl.CostEstimate(
            flops=flops, bytes_accessed=2 * (3 * J * D * F + A * D), transcendentals=rows * F * J
        ),
    )(
        out_grad, layer_input, norm_gain[None, :], routes, gates, gp, up,
        w_gate, w_up, w_down, w_out,
    )
    return (resid[None], head[None])


def solution(mesh):
    placed = (
        P(("exp", "head"), None),
        P(("exp", "head"), None),
        P(),
        P(("exp", "head"), None),
        P(("exp", "head"), None),
        P("head", "exp", None, None, "seq"),
        P("head", "exp", None, None, "seq"),
        P("exp", None, "seq"),
        P("exp", None, "seq"),
        P("exp", "seq", None),
        P("head", None),
    )
    return jax.shard_map(
        shards,
        mesh=mesh,
        in_specs=placed,
        out_specs=(P("seq", ("exp", "head"), None), P("seq", "exp", "head")),
        check_vma=False,
    )
```

time: 181 us -> 61.2 us (0.34)
  blocking collectives: 60.7 us -> 0 us
  waiting for transfers between devices: 58.8 us -> 0 us
  Pallas kernels: 0 us -> 54.4 us
  between operations: 14.2 us -> 0.64 us
  other arithmetic: 13.4 us -> 0 us
  local copies, waits for them, and re-layouts: 17.8 us -> 5.98 us
  matrix products: 10.6 us -> 0 us
  starting transfers between devices: 4.38 us -> 0 us
    all_to_all x1 -> x0, blocking collectives: 55.5 us -> none  [shards(): lax.all_to_all(outgoing, 'exp', split_axis=1, concat_axis=1, tiled=True)]
    pallas_call x0 -> x1, Pallas kernels: none -> 54.4 us  [shards(): pl.pallas_call(functools.partial(kernel, (S, E, H, J, T, D, C)), out_shap...]
    all_to_all x1 -> x0, waiting for transfers between devices: 49 us -> none  [shards(): lax.all_to_all(partial_value, 'exp', split_axis=1, concat_axis=1, tiled=T...]
    dot_general x4 -> x0, matrix products: 10.6 us -> none  [the longest x1 6.69 us: shards(): lax.dot_general(lax.all_gather(rounded_grad, 'head', axis=0, tiled=True),...]
    reduce_scatter x1 -> x0, waiting for transfers between devices: 9.83 us -> none  [shards(): lax.psum_scatter(combined.astype(jnp.bfloat16), 'seq', scatter_dimension=...]
    gather x1 -> x0, local copies, waits for them, and re-layouts: 6.97 us -> none  [shards(): picked = returned[slot_index].astype(jnp.float32)]
    all_gather x1 -> x0, blocking collectives: 5.28 us -> none  [shards(): lax.all_gather(rounded_grad, 'head', axis=0, tiled=True)]
    reduce_sum x4 -> x0, other arithmetic: 5.27 us -> none  [the longest x1 3.2 us: shards(): jnp.sum(picked.reshape(tok_count, top_count, model_width), axis=1)]
  transfers between devices with their start and end apart: 2 -> 0, of which waited for: 2 -> 0; matrix products, arithmetic and copies ran while one was open for 0% -> 0% of each run, Pallas kernels for 0% -> 0%
where the time goes in v1:
time: 61.2 us; the launch traced here: 61 us
  Pallas kernels  54.4 us (89%)
  local copies, waits for them, and re-layouts  5.98 us (10%)
  between operations  0.64 us (1%)
    pallas_call x1, Pallas kernels, shards(): pl.pallas_call(functools.partial(kernel, (S, E, H, J, T, D, C)), out_shap...  54.4 us
    unnamed x4, local copies, waits for them, and re-layouts  5.98 us

profile of v1, /device:TPU:0, one launch (start us, length us, event | category | flops | bytes accessed | tf_op | source)
XLA Modules:
  0.0 61.0 jit_solution(3422934579546716066)
XLA Ops:
  0.6 1.4 %copy.13.routes = s32[48,8]{1,0:T(8,128)} copy(s32[48,8]{0,1:T(8,128)} %param.14) | data formatting | bytes 3072 | tf_op args[3]
  2.0 1.4 %copy.14.gates = f32[48,8]{1,0:T(8,128)} copy(f32[48,8]{0,1:T(8,128)} %param.15) | data formatting | bytes 3072 | tf_op args[4]
  3.4 54.4 %shard_map.122 = (f32[24,2048]{1,0:T(8,128)}, bf16[48,2048]{1,0:T(8,128)(2,1)}) custom-call(bf16[48,2048]{1,0:T(8,128)(2,1)} %og.1, bf16[48,2048]{1,0:T(8,128)(2,1)} %li.1, f32[1,2048]{1,0:T(1,128)} %bitcast.9, s32[48,8]{1,0:T(8,128)} %copy.13.routes, f32[48,8]{1,0:T(8,128)} %copy.14.gates, bf16[2,256,384]{2,1,0:T(8,128)(2,1)} %bitcast.5, ...), custom_call_target="tpu_custom_call" | custom-call | flops 4026531840 | bytes 17825792 | tf_op jit(solution)/shard_map/pallas_call | solution.py:301
  57.7 1.6 %copy.17 = f32[1,24,2048]{2,1,0:T(8,128)} copy(f32[1,24,2048]{2,1,0:T(8,128)} %bitcast.8) | data formatting | bytes 393216
  59.4 1.6 %copy.18 = bf16[1,48,2048]{2,1,0:T(8,128)(2,1)} copy(bf16[1,48,2048]{2,1,0:T(8,128)(2,1)} %bitcast.7) | data formatting | bytes 393216

commit v2 on v1

--- a/solution.py
+++ b/solution.py
@@ -11,7 +11,7 @@
 F32 = jnp.float32
 BF16 = jnp.bfloat16
 NT_DIMS = (((1,), (1,)), ((), ()))
-COLUMN_TILES = 4
+LANES = 128
 
 
 def dot_nt(a, b):
@@ -23,7 +23,7 @@
     og, li, gain, routes, gates, gp_hbm, up_hbm, wg_hbm, wu_hbm, wd_hbm, wo_hbm,
     resid, head,
     xg, info_src, info_all, gp, up, wg, wu, wd, wo, coef_gate, coef_up, dgate, dup,
-    mine, core_rx, sx, x_rx, sz, z_rx, moe, hx, lhs,
+    mine, core_rx, sx, x_rx, sz, z_rx, moe, normed, hx, lhs,
     load_sem, z_snd, sib_snd, x_snd, info_snd, core_snd, xs_snd, zs_snd, head_snd,
     xg_rcv, info_rcv, core_rcv, xs_rcv, zs_rcv, head_rcv,
 ):
@@ -31,8 +31,9 @@
     Z = E // 2
     DS = D // S
     R = T // S
-    NT = COLUMN_TILES
-    TN = DS // NT
+    F = wd.shape[1]
+    TN = LANES
+    NT = DS // TN
     s = lax.axis_index("seq")
     e = lax.axis_index("exp")
     h = lax.axis_index("head")
@@ -45,6 +46,13 @@
             src_ref=src, dst_ref=dst, send_sem=snd, recv_sem=rcv,
             device_id=where, device_id_type=MESH,
         )
+
+    def rows_of(ref):
+        wide = ref[...].astype(F32)
+        mine_rows = wide[:R]
+        for p in range(1, S):
+            mine_rows = jnp.where(s == p, wide[p * R:(p + 1) * R], mine_rows)
+        return mine_rows
 
     barrier = pltpu.get_barrier_semaphore()
     for k in range(1, E):
@@ -65,6 +73,26 @@
     for q in range(S):
         xg[e, q] = og[:, q * DS:(q + 1) * DS]
 
+    X8 = E * 8
+    XP = max(LANES, X8)
+    line = lax.broadcasted_iota(jnp.int32, (X8, T), 0)
+    kind = line % 8
+    expert = (line // 8) * J + kind % J
+    weight = jnp.zeros((X8, T), F32)
+    member = jnp.zeros((X8, T), F32)
+    for k in range(routes.shape[0]):
+        hit = routes[k:k + 1, :] == expert
+        weight = weight + jnp.where(hit, gates[k:k + 1, :], 0.0)
+        member = jnp.where(hit, 1.0, member)
+    earlier = (
+        lax.broadcasted_iota(jnp.int32, (T, T), 0) < lax.broadcasted_iota(jnp.int32, (T, T), 1)
+    ).astype(F32).astype(BF16)
+    position = jnp.dot(member.astype(BF16), earlier, preferred_element_type=F32)
+    info = jnp.where(kind < J, weight, jnp.where(member > 0.0, position, -1.0))
+    info_src[...] = jnp.zeros((E, 8, LANES), F32)
+    info_src[:, :, :T] = info.reshape(E, 8, T)
+    info_all[e] = info_src[e]
+
     pl.semaphore_wait(barrier, E - 1 + S - 1 + H - 1)
 
     sent = []
@@ -76,33 +104,45 @@
     def chunk(block, part, snd, **where):
         return remote(xg.at[block, part], xg.at[block, part], snd, xg_rcv.at[block, part], **where)
 
+    for k in range(1, E):
+        to = (e + k) % E
+        start(remote(info_src.at[to], info_all.at[e], info_snd.at[k], info_rcv.at[e], exp=to))
     for k in range(1, Z):
         start(chunk(e, s, z_snd.at[k], exp=((z + k) % Z) * 2 + c))
     for q in range(S):
         start(chunk(e, q, sib_snd.at[0, q], exp=sib))
 
-    X8 = E * 8
-    XP = max(128, X8)
-    lane = lax.broadcasted_iota(jnp.int32, (T, XP), 1)
-    kind = lane % 8
-    expert = (lane // 8) * J + kind % J
-    weight = jnp.zeros((T, XP), F32)
-    member = jnp.zeros((T, XP), F32)
-    for k in range(routes.shape[1]):
-        hit = routes[:, k:k + 1] == expert
-        weight = weight + jnp.where(hit, gates[:, k:k + 1], 0.0)
-        member = jnp.where(hit, 1.0, member)
-    earlier = (
-        lax.broadcasted_iota(jnp.int32, (T, T), 0) > lax.broadcasted_iota(jnp.int32, (T, T), 1)
-    ).astype(F32).astype(BF16)
-    position = jnp.dot(earlier, member.astype(BF16), preferred_element_type=F32)
-    info = jnp.where(kind < J, weight, jnp.where(member > 0.0, position, -1.0))
-    info = jnp.concatenate([info, jnp.zeros((128 - T, XP), F32)], axis=0).T
-    info_src[...] = info[:X8].reshape(E, 8, 128)
+    inputs = rows_of(li)
+    inv_rms = lax.rsqrt(jnp.mean(inputs * inputs, axis=1, keepdims=True) + 1e-06)
+    normed[...] = inputs * inv_rms
+
     for k in range(1, E):
-        to = (e + k) % E
-        start(remote(info_src.at[to], info_all.at[e], info_snd.at[k], info_rcv.at[e], exp=to))
-    info_all[e] = info_src[e]
+        frm = (e + k) % E
+        remote(info_src.at[frm], info_all.at[frm], info_snd.at[k], info_rcv.at[frm], exp=frm).wait_recv()
+    loads[0].wait()
+    loads[1].wait()
+
+    def slot_values(experts):
+        table = info_all[...].reshape(X8, LANES)
+        if XP > X8:
+            table = jnp.concatenate([table, jnp.zeros((XP - X8, LANES), F32)], axis=0)
+        table = table.T
+        slot = lax.broadcasted_iota(jnp.int32, (E * T, E * C), 1).astype(F32)
+        for j in experts:
+            gate_col = jnp.concatenate([table[:T, b * 8 + j:b * 8 + j + 1] for b in range(E)], axis=0)
+            place = []
+            for b in range(E):
+                col = table[:T, b * 8 + J + j:b * 8 + J + j + 1]
+                place.append(jnp.where(col >= 0.0, col + float(b * C), -1.0))
+            place = jnp.concatenate(place, axis=0)
+            pick = jnp.where(slot == place, 1.0, 0.0).astype(BF16)
+            a = jnp.dot(pick, gp[j], preferred_element_type=F32)
+            b = jnp.dot(pick, up[j], preferred_element_type=F32)
+            sig = jax.nn.sigmoid(a)
+            coef_gate[j] = gate_col * b * sig * (1.0 + a * (1.0 - sig))
+            coef_up[j] = gate_col * a * sig
+
+    slot_values(range(1))
 
     for k in range(1, Z):
         block = ((z + k) % Z) * 2 + c
@@ -111,29 +151,7 @@
             start(chunk(block, s, x_snd.at[k, i], seq=(s + i) % S))
         start(chunk(block, s, sib_snd.at[k, 0], exp=sib))
 
-    for k in range(1, E):
-        frm = (e + k) % E
-        remote(info_src.at[frm], info_all.at[frm], info_snd.at[k], info_rcv.at[frm], exp=frm).wait_recv()
-    table = info_all[...].reshape(X8, 128)
-    if XP > X8:
-        table = jnp.concatenate([table, jnp.zeros((XP - X8, 128), F32)], axis=0)
-    table = table.T
-    loads[0].wait()
-    loads[1].wait()
-    slot = lax.broadcasted_iota(jnp.int32, (E * T, E * C), 1).astype(F32)
-    for j in range(J):
-        gate_col = jnp.concatenate([table[:T, b * 8 + j:b * 8 + j + 1] for b in range(E)], axis=0)
-        place = []
-        for b in range(E):
-            col = table[:T, b * 8 + J + j:b * 8 + J + j + 1]
-            place.append(jnp.where(col >= 0.0, col + float(b * C), -1.0))
-        place = jnp.concatenate(place, axis=0)
-        pick = jnp.where(slot == place, 1.0, 0.0).astype(BF16)
-        a = jnp.dot(pick, gp[j], preferred_element_type=F32)
-        b = jnp.dot(pick, up[j], preferred_element_type=F32)
-        sig = jax.nn.sigmoid(a)
-        coef_gate[j] = gate_col * b * sig * (1.0 + a * (1.0 - sig))
-        coef_up[j] = gate_col * a * sig
+    slot_values(range(1, J))
 
     for k in range(1, Z):
         block = ((z + k) % Z) * 2 + c
@@ -149,13 +167,15 @@
             chunk(block, part, sib_snd.at[k, i], exp=sib).wait_recv()
 
     loads[2].wait()
+    hidden = None
+    for q in range(S):
+        down = wd[:, :, q * DS:(q + 1) * DS].reshape(J * F, DS)
+        term = dot_nt(xg[:, q].reshape(E * T, DS), down)
+        hidden = term if hidden is None else hidden + term
     for j in range(J):
-        hidden = None
-        for q in range(S):
-            term = dot_nt(xg[:, q].reshape(E * T, DS), wd[j, :, q * DS:(q + 1) * DS])
-            hidden = term if hidden is None else hidden + term
-        dgate[j] = (hidden * coef_gate[j]).astype(BF16)
-        dup[j] = (hidden * coef_up[j]).astype(BF16)
+        here = hidden[:, j * F:(j + 1) * F]
+        dgate[j] = (here * coef_gate[j]).astype(BF16)
+        dup[j] = (here * coef_up[j]).astype(BF16)
     loads[3].wait()
     loads[4].wait()
 
@@ -171,14 +191,18 @@
         return remote(sz.at[n, to], z_rx.at[n, k], zs_snd.at[n, k], zs_rcv.at[n, k], exp=to * 2 + c)
 
     def stage_compute(n):
-        tiles = []
-        for q in range(S):
-            cols = slice(q * DS + n * TN, q * DS + (n + 1) * TN)
-            acc = None
-            for j in range(J):
-                term = dot_nt(dgate[j], wg[j, cols, :]) + dot_nt(dup[j], wu[j, cols, :])
-                acc = term if acc is None else acc + term
-            tiles.append(acc)
+        bands = [slice(q * DS + n * TN, q * DS + (n + 1) * TN) for q in range(S)]
+
+        def weights(ref, j):
+            return jnp.concatenate([ref[j, band, :] for band in bands], axis=0)
+
+        left = [ref[j] for j in range(J) for ref in (dgate, dup)]
+        right = [weights(ref, j) for j in range(J) for ref in (wg, wu)]
+        if F % LANES == 0:
+            acc = dot_nt(jnp.concatenate(left, axis=1), jnp.concatenate(right, axis=1))
+        else:
+            acc = sum(dot_nt(lt, rt) for lt, rt in zip(left, right))
+        tiles = [acc[:, q * TN:(q + 1) * TN] for q in range(S)]
         for b in range(E):
             for p in range(S):
                 rows = slice(b * T + p * R, b * T + (p + 1) * R)
@@ -210,25 +234,21 @@
         for q in range(S):
             moe[:, q * DS + n * TN:q * DS + (n + 1) * TN] = total[q * R:(q + 1) * R]
 
-    stages = (stage_compute, stage_x, stage_z, stage_end)
-    for step in range(NT + len(stages) - 1):
-        for i, stage in enumerate(stages):
-            if 0 <= step - i < NT:
-                stage(step - i)
-
-    def rows_of(ref):
-        wide = ref[...].astype(F32)
-        mine_rows = wide[:R]
-        for p in range(1, S):
-            mine_rows = jnp.where(s == p, wide[p * R:(p + 1) * R], mine_rows)
-        return mine_rows
-
-    inputs = rows_of(li)
-    inv_rms = lax.rsqrt(jnp.mean(inputs * inputs, axis=1, keepdims=True) + 1e-06)
-    normed = inputs * inv_rms
+    for n in range(NT):
+        stage_compute(n)
+        if n >= 1:
+            stage_x(n - 1)
+        if n >= 5:
+            stage_z(n - 5)
+    stage_x(NT - 1)
+    for n in range(max(NT - 5, 0), NT):
+        stage_z(n)
+    for n in range(NT):
+        stage_end(n)
+
     scaled = moe[...] * gain[...]
     full = rows_of(og) + inv_rms * (
-        scaled - normed * jnp.mean(scaled * normed, axis=1, keepdims=True)
+        scaled - normed[...] * jnp.mean(scaled * normed[...], axis=1, keepdims=True)
     )
     resid[...] = full
     hx[h] = jnp.concatenate([full[:, q * DS:(q + 1) * DS] for q in range(S)], axis=0).astype(BF16)
@@ -251,6 +271,17 @@
         copy.wait_send()
 
 
+def publish(resid, head, resid_out, head_out, sem):
+    copies = [
+        pltpu.make_async_copy(resid, resid_out, sem.at[0]),
+        pltpu.make_async_copy(head, head_out, sem.at[1]),
+    ]
+    for copy in copies:
+        copy.start()
+    for copy in copies:
+        copy.wait()
+
+
 def shards(
     out_grad, layer_input, norm_gain, routes, gates, gate_pre, up_pre, w_gate, w_up, w_down, w_out
 ):
@@ -262,8 +293,8 @@
     Z = E // 2
     DS = D // S
     R = T // S
-    NT = COLUMN_TILES
-    TN = DS // NT
+    TN = LANES
+    NT = DS // TN
     gp = gate_pre.reshape(J, E * C, F)
     up = up_pre.reshape(J, E * C, F)
     vmem = pl.BlockSpec(memory_space=pltpu.VMEM)
@@ -290,6 +321,7 @@
         pltpu.VMEM((NT, Z, T, TN), BF16),
         pltpu.VMEM((NT, Z, T, TN), BF16),
         pltpu.VMEM((R, D), F32),
+        pltpu.VMEM((R, D), F32),
         pltpu.VMEM((H, T, DS), BF16),
         pltpu.VMEM((H * R, D), BF16),
         dma((6,)), dma((Z,)), dma((Z, S)), dma((Z, S)), dma((E,)), dma((NT,)),
@@ -314,9 +346,19 @@
             flops=flops, bytes_accessed=2 * (3 * J * D * F + A * D), transcendentals=rows * F * J
         ),
     )(
-        out_grad, layer_input, norm_gain[None, :], routes, gates, gp, up,
+        out_grad, layer_input, norm_gain[None, :], routes.T, gates.T, gp, up,
         w_gate, w_up, w_down, w_out,
     )
+    resid, head = pl.pallas_call(
+        publish,
+        out_shape=(
+            jax.ShapeDtypeStruct(resid.shape, F32),
+            jax.ShapeDtypeStruct(head.shape, BF16),
+        ),
+        in_specs=[hbm, hbm],
+        out_specs=(hbm, hbm),
+        scratch_shapes=[dma((2,))],
+    )(resid, head)
     return (resid[None], head[None])
 
 

time: 61.2 us -> 65.7 us (1.074)
  Pallas kernels: 54.4 us -> 64.9 us
  local copies, waits for them, and re-layouts: 5.98 us -> 0 us
    pallas_call x0 -> x1, Pallas kernels: none -> 13 us  [shards(): pl.pallas_call(publish, out_shape=(jax.ShapeDtypeStruct(resid.shape, F32)...]
    unnamed x4 -> x0, local copies, waits for them, and re-layouts: 5.98 us -> none
    pallas_call x1, Pallas kernels: 54.4 us -> 51.8 us  [shards(): pl.pallas_call(functools.partial(kernel, (S, E, H, J, T, D, C)), out_shap...]
where the time goes in v2:
time: 65.7 us; the launch traced here: 65.5 us
  Pallas kernels  64.9 us (99%)
    pallas_call x1, Pallas kernels, shards(): pl.pallas_call(functools.partial(kernel, (S, E, H, J, T, D, C)), out_shap...  51.8 us
    pallas_call x1, Pallas kernels, shards(): pl.pallas_call(publish, out_shape=(jax.ShapeDtypeStruct(resid.shape, F32)...  13 us

profile of v2, /device:TPU:0, one launch (start us, length us, event | category | flops | bytes accessed | tf_op | source)
XLA Modules:
  0.0 65.5 jit_solution(5861650492749606656)
XLA Ops:
  0.6 51.8 %shard_map.122 = (f32[24,2048]{1,0:T(8,128)}, bf16[48,2048]{1,0:T(8,128)(2,1)}) custom-call(bf16[48,2048]{1,0:T(8,128)(2,1)} %og.1, bf16[48,2048]{1,0:T(8,128)(2,1)} %li.1, f32[1,2048]{1,0:T(1,128)} %bitcast.9, s32[8,48]{1,0:T(8,128)} %bitcast.10, f32[8,48]{1,0:T(8,128)} %bitcast.11, bf16[2,256,384]{2,1,0:T(8,128)(2,1)} %bitcast.7, ...), custom_call_target="tpu_custom_call" | custom-call | flops 4026531840 | bytes 17825792 | tf_op jit(solution)/shard_map/pallas_call | solution.py:333
  52.5 13.0 %shard_map.123 = (f32[24,2048]{1,0:T(8,128)}, bf16[48,2048]{1,0:T(8,128)(2,1)}) custom-call(f32[24,2048]{1,0:T(8,128)} %get-tuple-element.6.resid, bf16[48,2048]{1,0:T(8,128)(2,1)} %get-tuple-element.7.head), custom_call_target="tpu_custom_call" | custom-call | tf_op jit(solution)/shard_map/pallas_call | solution.py:352

commit v3 on v2

--- a/solution.py
+++ b/solution.py
@@ -68,7 +68,7 @@
             ((gp_hbm, gp), (up_hbm, up), (wd_hbm, wd), (wg_hbm, wg), (wu_hbm, wu), (wo_hbm, wo))
         )
     ]
-    for load in loads:
+    for load in loads[:3]:
         load.start()
     for q in range(S):
         xg[e, q] = og[:, q * DS:(q + 1) * DS]
@@ -95,6 +95,15 @@
 
     pl.semaphore_wait(barrier, E - 1 + S - 1 + H - 1)
 
+    room = jnp.minimum(z, Z - 1 - z)
+    longer = jnp.where(2 * z < Z, 1, -1)
+
+    def nearest(k):
+        both = (k + 1) // 2 * (1 if k % 2 else -1)
+        return z + longer * jnp.where(k <= 2 * room, both, k - room)
+
+    order = [z] + [nearest(k) for k in range(1, Z)]
+
     sent = []
 
     def start(copy):
@@ -108,9 +117,12 @@
         to = (e + k) % E
         start(remote(info_src.at[to], info_all.at[e], info_snd.at[k], info_rcv.at[e], exp=to))
     for k in range(1, Z):
-        start(chunk(e, s, z_snd.at[k], exp=((z + k) % Z) * 2 + c))
+        start(chunk(e, s, z_snd.at[k], exp=order[k] * 2 + c))
     for q in range(S):
         start(chunk(e, q, sib_snd.at[0, q], exp=sib))
+
+    for load in loads[3:]:
+        load.start()
 
     inputs = rows_of(li)
     inv_rms = lax.rsqrt(jnp.mean(inputs * inputs, axis=1, keepdims=True) + 1e-06)
@@ -145,7 +157,7 @@
     slot_values(range(1))
 
     for k in range(1, Z):
-        block = ((z + k) % Z) * 2 + c
+        block = order[k] * 2 + c
         chunk(block, s, z_snd.at[k], exp=sib).wait_recv()
         for i in range(1, S):
             start(chunk(block, s, x_snd.at[k, i], seq=(s + i) % S))
@@ -154,14 +166,14 @@
     slot_values(range(1, J))
 
     for k in range(1, Z):
-        block = ((z + k) % Z) * 2 + c
+        block = order[k] * 2 + c
         for i in range(1, S):
             part = (s + S - i) % S
             chunk(block, part, x_snd.at[k, i], exp=sib).wait_recv()
             start(chunk(block, part, sib_snd.at[k, i], exp=sib))
 
     for k in range(Z):
-        block = ((z + k) % Z) * 2 + (1 - c)
+        block = order[k] * 2 + (1 - c)
         for i in range(S):
             part = (s + S - i) % S
             chunk(block, part, sib_snd.at[k, i], exp=sib).wait_recv()
@@ -271,14 +283,21 @@
         copy.wait_send()
 
 
-def publish(resid, head, resid_out, head_out, sem):
-    copies = [
-        pltpu.make_async_copy(resid, resid_out, sem.at[0]),
-        pltpu.make_async_copy(head, head_out, sem.at[1]),
+def publish(resid, head, resid_out, head_out, resid_v, head_v, sem):
+    arrive = [
+        pltpu.make_async_copy(head, head_v, sem.at[0]),
+        pltpu.make_async_copy(resid, resid_v, sem.at[1]),
     ]
-    for copy in copies:
+    leave = [
+        pltpu.make_async_copy(head_v, head_out, sem.at[2]),
+        pltpu.make_async_copy(resid_v, resid_out, sem.at[3]),
+    ]
+    for copy in arrive:
         copy.start()
-    for copy in copies:
+    for first, second in zip(arrive, leave):
+        first.wait()
+        second.start()
+    for copy in leave:
         copy.wait()
 
 
@@ -357,7 +376,9 @@
         ),
         in_specs=[hbm, hbm],
         out_specs=(hbm, hbm),
-        scratch_shapes=[dma((2,))],
+        scratch_shapes=[
+            pltpu.VMEM(resid.shape, F32), pltpu.VMEM(head.shape, BF16), dma((4,))
+        ],
     )(resid, head)
     return (resid[None], head[None])
 

time: 65.7 us -> 53.5 us (0.81)
  Pallas kernels: 64.9 us -> 52.7 us
    pallas_call x1, Pallas kernels: 13 us -> 1.73 us  [shards(): pl.pallas_call(publish, out_shape=(jax.ShapeDtypeStruct(resid.shape, F32)...]
    pallas_call x1, Pallas kernels: 51.8 us -> 51 us  [shards(): pl.pallas_call(functools.partial(kernel, (S, E, H, J, T, D, C)), out_shap...]
where the time goes in v3:
time: 53.5 us; the launch traced here: 53.4 us
  Pallas kernels  52.7 us (99%)
  between operations  0.64 us (1%)
    pallas_call x1, Pallas kernels, shards(): pl.pallas_call(functools.partial(kernel, (S, E, H, J, T, D, C)), out_shap...  51 us
    pallas_call x1, Pallas kernels, shards(): pl.pallas_call(publish, out_shape=(jax.ShapeDtypeStruct(resid.shape, F32)...  1.73 us

profile of v3, /device:TPU:0, one launch (start us, length us, event | category | flops | bytes accessed | tf_op | source)
XLA Modules:
  0.0 53.4 jit_solution(11124906241487840601)
XLA Ops:
  0.6 51.0 %shard_map.122 = (f32[24,2048]{1,0:T(8,128)}, bf16[48,2048]{1,0:T(8,128)(2,1)}) custom-call(bf16[48,2048]{1,0:T(8,128)(2,1)} %og.1, bf16[48,2048]{1,0:T(8,128)(2,1)} %li.1, f32[1,2048]{1,0:T(1,128)} %bitcast.9, s32[8,48]{1,0:T(8,128)} %bitcast.10, f32[8,48]{1,0:T(8,128)} %bitcast.11, bf16[2,256,384]{2,1,0:T(8,128)(2,1)} %bitcast.7, ...), custom_call_target="tpu_custom_call" | custom-call | flops 4026531840 | bytes 17825792 | tf_op jit(solution)/shard_map/pallas_call | solution.py:352
  51.6 1.7 %shard_map.123 = (f32[24,2048]{1,0:T(8,128)}, bf16[48,2048]{1,0:T(8,128)(2,1)}) custom-call(f32[24,2048]{1,0:T(8,128)} %get-tuple-element.6.resid, bf16[48,2048]{1,0:T(8,128)(2,1)} %get-tuple-element.7.head), custom_call_target="tpu_custom_call" | custom-call | tf_op jit(solution)/shard_map/pallas_call | solution.py:371
